TPU v7x, 256 devices: a whole 4x4x8 slice. The times are simulated.
256 devices in a mesh: col: 64 (over z, y, core), row: 4 (over x).
Axes of the slice: x: 4, y: 4, z: 8, core: 2. Of those that a mesh axis runs over, the one named last changes fastest.
Arguments:
- right_side: float32 [8192, 256], P(('row', 'col')), may hold values from -6 to 6
- prior_solution: bfloat16 [131072, 256], P('col'), may hold values from -6 to 6
- factor_codes: bfloat16 [8192, 131072], P('row', 'col'), may hold values from -0.015625 to 0.015625
- block_scale: float32 [4, 512], P('row', 'col'), may hold values from 0.3 to 3
- diag_inverse: bfloat16 [4, 2048, 2048], P('row', 'col'), may hold values from -0.125 to 0.125
- inner_factor: bfloat16 [4, 4, 2048, 2048], P('row', None, 'col'), may hold values from -0.125 to 0.125
Outputs:
- solved: float32 [8192, 256], P(('row', 'col'))
All inputs are finite; a program needn't handle non-finite values.
Results may differ from a plain program's by a relative error of at most 0.0095.
Values may be sent and summed in bfloat16 or wider, within the bound.
A program may use at most 64 MiB of HBM per device.

v0:
```python
import jax
import jax.numpy as jnp
from jax import lax
from jax.sharding import PartitionSpec as P


def cut_along(x, dim, length):
    before, after = (x.shape[:dim], x.shape[dim + 1 :])
    return jnp.moveaxis(x.reshape(*before, length, -1, *after), dim, 0)


def sent_and_summed(x, axis, dim):
    length = lax.axis_size(axis)
    pieces = lax.all_to_all(cut_along(x, dim, length), axis, 0, 0, tiled=True)
    return jnp.sum(pieces, axis=0)


def copy_for_each(x, axis):
    length = lax.axis_size(axis)
    return lax.all_to_all(jnp.broadcast_to(x[None], (length, *x.shape)), axis, 0, 0, tiled=True)


def in_order(pieces, dim):
    pieces = jnp.moveaxis(pieces, 0, dim)
    dims = pieces.shape
    return pieces.reshape(*dims[:dim], dims[dim] * dims[dim + 1], *dims[dim + 2 :])


def collect(x, axis, dim):
    pieces = copy_for_each(x, axis)
    return in_order(pieces, dim)


def from_root(x, axis, root):
    return lax.dynamic_index_in_dim(lax.all_gather(x, axis), root, 0, keepdims=False)


def local(right_side, prior_solution, factor_codes, block_scale, diag_inverse, inner_factor):
    rows_each = right_side.shape[0]
    blocks_here = block_scale.shape[1]
    block_cols = factor_codes.shape[1] // blocks_here
    columns_out = right_side.shape[1]
    summed = jnp.zeros((rows_each * lax.axis_size("col"), columns_out), jnp.float32)
    for column_block in range(blocks_here):
        coded = lax.dynamic_slice(
            factor_codes,
            (0, column_block * block_cols),
            (rows_each * lax.axis_size("col"), block_cols),
        )
        earlier = prior_solution[column_block * block_cols : (column_block + 1) * block_cols]
        summed = summed + block_scale[0, column_block] * jnp.dot(
            coded, earlier, preferred_element_type=jnp.float32
        )
    prior_rows = sent_and_summed(summed, "col", 0)
    rhs = right_side - prior_rows
    row_place = lax.axis_index("row")
    solved = jnp.zeros((rows_each, columns_out), jnp.float32)
    empty = jnp.zeros((rows_each, columns_out), jnp.float32)
    inverse_rows = diag_inverse[0]
    panel_count = lax.axis_size("row")
    for section in range(panel_count):
        rounded = rhs.astype(jnp.bfloat16)
        whole_rhs = collect(rounded, "col", 0)
        current = jnp.dot(inverse_rows, whole_rhs, preferred_element_type=jnp.float32)
        solved = jnp.where(row_place == section, current, solved)
        if section + 1 < panel_count:
            sending = current.astype(jnp.bfloat16)
            coupling = inner_factor[0, section]
            arrived = from_root(sending, "row", section)

            def apply_coupling(running, portion, offset, coupling=coupling):
                return jnp.dot(coupling, portion, preferred_element_type=jnp.float32)

            update = apply_coupling(empty, collect(arrived, "col", 0), jnp.int32(0))
            rhs = rhs - jnp.where(row_place > section, update, 0.0)
    return solved


def solution(mesh):
    return jax.shard_map(
        local,
        mesh=mesh,
        in_specs=(
            P(("row", "col"), None),
            P("col", None),
            P("row", "col"),
            P("row", "col"),
            P("row", "col", None),
            P("row", None, "col", None),
        ),
        out_specs=P(("row", "col"), None),
        check_vma=False,
    )
```

profile of v0, /device:TPU:7, one launch (start us, length us, event | category | flops | bytes accessed | tf_op | source)
XLA Modules:
  0.0 361.0 jit_solution(565850219860232735)
XLA Ops:
  0.0 1.6 fusion.45
  1.6 2.6 convolution_multiply_fusion.7
  4.3 2.5 fusion.6
  6.8 2.0 fusion.5
  8.8 1.1 fusion.4
  9.9 1.1 fusion.3
  10.9 1.1 fusion.2
  12.0 1.0 fusion.1
  13.0 1.1 fusion
  14.1 61.8 %all_to_all.40 = f32[64,32,256]{2,1,0:T(8,128)S(1)} all-to-all(f32[64,32,256]{2,1,0:T(8,128)S(1)} %bitcast.67), channel_id=1, replica_groups=mesh['col'=64,'row'=4] {'col'}, dimensions={0} | all-to-all | bytes 4194304 | tf_op jit(solution)/shard_map/all_to_all | solution.py:14
  76.1 0.6 copy-done.4
  76.8 34.8 %all_to_all.41 = bf16[64,32,256]{2,1,0:T(8,128)(2,1)S(1)} all-to-all(bf16[64,32,256]{2,1,0:T(8,128)(2,1)S(1)} %broadcast_in_dim.26), channel_id=1, replica_groups=mesh['col'=64,'row'=4] {'col'}, dimensions={0} | all-to-all | bytes 2097152 | tf_op jit(solution)/shard_map/all_to_all | solution.py:20
  111.9 9.0 %all-gather = bf16[128,256]{1,0:T(8,128)(2,1)S(1)} all-gather(bf16[32,256]{1,0:T(8,128)(2,1)S(1)} %convert_bitcast_fusion.2), channel_id=2, replica_groups=mesh['col'=64,'row'=4] {'row'}, dimensions={0}, use_global_device_ids=true | all-gather | bytes 81920 | tf_op jit(solution)/shard_map/all_gather | solution.py:35
  120.9 1.1 broadcast_in_dim.28
  122.0 9.4 %all-to-all-start.2 = ((bf16[64,32,256]{2,1,0:T(8,128)(2,1)}), bf16[64,32,256]{2,1,0:T(8,128)(2,1)S(1)}, u32[]{:S(2)}, u32[]{:S(2)}) async-start(bf16[64,32,256]{2,1,0:T(8,128)(2,1)} %broadcast_in_dim.28), calls=%async_computation.2 | async-start | bytes 2097152 | tf_op jit(solution)/shard_map/all_to_all | solution.py:20
  131.4 28.0 %all-to-all-done.2 = bf16[64,32,256]{2,1,0:T(8,128)(2,1)S(1)} async-done(((bf16[64,32,256]{2,1,0:T(8,128)(2,1)}), bf16[64,32,256]{2,1,0:T(8,128)(2,1)S(1)}, u32[]{:S(2)}, u32[]{:S(2)}) %all-to-all-start.2) | async-done | bytes 1048608 | tf_op jit(solution)/shard_map/all_to_all | solution.py:20
  159.4 0.3 fusion.46
  159.8 34.2 %all_to_all.42 = bf16[64,32,256]{2,1,0:T(8,128)(2,1)S(1)} all-to-all(bf16[64,32,256]{2,1,0:T(8,128)(2,1)S(1)} %broadcast_in_dim.30), channel_id=1, replica_groups=mesh['col'=64,'row'=4] {'col'}, dimensions={0} | all-to-all | bytes 2097152 | tf_op jit(solution)/shard_map/all_to_all | solution.py:20
  194.4 9.0 %all-gather.1 = bf16[128,256]{1,0:T(8,128)(2,1)S(1)} all-gather(bf16[32,256]{1,0:T(8,128)(2,1)S(1)} %convert_bitcast_fusion.1), channel_id=3, replica_groups=mesh['col'=64,'row'=4] {'row'}, dimensions={0}, use_global_device_ids=true | all-gather | bytes 81920 | tf_op jit(solution)/shard_map/all_gather | solution.py:35
  203.3 1.1 broadcast_in_dim.61
  204.4 9.3 %all-to-all-start.4 = ((bf16[64,32,256]{2,1,0:T(8,128)(2,1)}), bf16[64,32,256]{2,1,0:T(8,128)(2,1)S(1)}, u32[]{:S(2)}, u32[]{:S(2)}) async-start(bf16[64,32,256]{2,1,0:T(8,128)(2,1)} %broadcast_in_dim.61), calls=%async_computation.4 | async-start | bytes 2097152 | tf_op jit(solution)/shard_map/all_to_all | solution.py:20
  213.8 28.0 %all-to-all-done.4 = bf16[64,32,256]{2,1,0:T(8,128)(2,1)S(1)} async-done(((bf16[64,32,256]{2,1,0:T(8,128)(2,1)}), bf16[64,32,256]{2,1,0:T(8,128)(2,1)S(1)}, u32[]{:S(2)}, u32[]{:S(2)}) %all-to-all-start.4) | async-done | bytes 1048608 | tf_op jit(solution)/shard_map/all_to_all | solution.py:20
  241.8 0.3 fusion.47
  242.2 34.2 %all_to_all.43 = bf16[64,32,256]{2,1,0:T(8,128)(2,1)S(1)} all-to-all(bf16[64,32,256]{2,1,0:T(8,128)(2,1)S(1)} %broadcast_in_dim.62), channel_id=1, replica_groups=mesh['col'=64,'row'=4] {'col'}, dimensions={0} | all-to-all | bytes 2097152 | tf_op jit(solution)/shard_map/all_to_all | solution.py:20
  276.8 9.0 %all-gather.2 = bf16[128,256]{1,0:T(8,128)(2,1)S(1)} all-gather(bf16[32,256]{1,0:T(8,128)(2,1)S(1)} %convert_bitcast_fusion), channel_id=4, replica_groups=mesh['col'=64,'row'=4] {'row'}, dimensions={0}, use_global_device_ids=true | all-gather | bytes 81920 | tf_op jit(solution)/shard_map/all_gather | solution.py:35
  285.7 1.1 broadcast_in_dim.64
  286.8 9.3 %all-to-all-start.6 = ((bf16[64,32,256]{2,1,0:T(8,128)(2,1)}), bf16[64,32,256]{2,1,0:T(8,128)(2,1)S(1)}, u32[]{:S(2)}, u32[]{:S(2)}) async-start(bf16[64,32,256]{2,1,0:T(8,128)(2,1)} %broadcast_in_dim.64), calls=%async_computation.6 | async-start | bytes 2097152 | tf_op jit(solution)/shard_map/all_to_all | solution.py:20
  296.2 28.0 %all-to-all-done.6 = bf16[64,32,256]{2,1,0:T(8,128)(2,1)S(1)} async-done(((bf16[64,32,256]{2,1,0:T(8,128)(2,1)}), bf16[64,32,256]{2,1,0:T(8,128)(2,1)S(1)}, u32[]{:S(2)}, u32[]{:S(2)}) %all-to-all-start.6) | async-done | bytes 1048608 | tf_op jit(solution)/shard_map/all_to_all | solution.py:20
  324.5 1.1 broadcast_in_dim.65
  325.6 6.5 %all-to-all-start.7 = ((bf16[64,32,256]{2,1,0:T(8,128)(2,1)}), bf16[64,32,256]{2,1,0:T(8,128)(2,1)S(1)}, u32[]{:S(2)}, u32[]{:S(2)}) async-start(bf16[64,32,256]{2,1,0:T(8,128)(2,1)} %broadcast_in_dim.65), calls=%async_computation.7 | async-start | bytes 2097152 | tf_op jit(solution)/shard_map/all_to_all | solution.py:20
  332.1 28.0 %all-to-all-done.7 = bf16[64,32,256]{2,1,0:T(8,128)(2,1)S(1)} async-done(((bf16[64,32,256]{2,1,0:T(8,128)(2,1)}), bf16[64,32,256]{2,1,0:T(8,128)(2,1)S(1)}, u32[]{:S(2)}, u32[]{:S(2)}) %all-to-all-start.7) | async-done | bytes 1048608 | tf_op jit(solution)/shard_map/all_to_all | solution.py:20
  360.1 0.9 fusion.7
  (24 shorter events, 1.7 us)
Async XLA Ops:
  0.0 111.6 %copy-start = (bf16[1,32,2048]{2,1,0:T(8,128)(2,1)S(1)}, bf16[1,32,2048]{2,1,0:T(8,128)(2,1)}, u32[]{:S(2)}) copy-start(bf16[1,32,2048]{2,1,0:T(8,128)(2,1)} %param.10) | copy-start | bytes 393220
  1.6 5.1 %copy-start.1 = (bf16[2048,2048]{1,0:T(8,128)(2,1)S(1)}, bf16[2048,2048]{1,0:T(8,128)(2,1)}, u32[]{:S(2)}) copy-start(bf16[2048,2048]{1,0:T(8,128)(2,1)} %param.8) | copy-start | bytes 25165828
  6.8 2.0 copy-start.2
  75.9 0.8 copy-start.4
  111.6 47.7 %copy-start.3 = (bf16[1,4,32,2048]{3,2,1,0:T(8,128)(2,1)S(1)}, bf16[1,4,32,2048]{3,2,1,0:T(8,128)(2,1)}, u32[]{:S(2)}) copy-start(bf16[1,4,32,2048]{3,2,1,0:T(8,128)(2,1)} %param.11) | copy-start | bytes 1572868
  122.0 37.3 %all-to-all-start.2 = ((bf16[64,32,256]{2,1,0:T(8,128)(2,1)}), bf16[64,32,256]{2,1,0:T(8,128)(2,1)S(1)}, u32[]{:S(2)}, u32[]{:S(2)}) async-start(bf16[64,32,256]{2,1,0:T(8,128)(2,1)} %broadcast_in_dim.28), calls=%async_computation.2 | async-start | bytes 2097152 | tf_op jit(solution)/shard_map/all_to_all | solution.py:20
  204.4 37.3 %all-to-all-start.4 = ((bf16[64,32,256]{2,1,0:T(8,128)(2,1)}), bf16[64,32,256]{2,1,0:T(8,128)(2,1)S(1)}, u32[]{:S(2)}, u32[]{:S(2)}) async-start(bf16[64,32,256]{2,1,0:T(8,128)(2,1)} %broadcast_in_dim.61), calls=%async_computation.4 | async-start | bytes 2097152 | tf_op jit(solution)/shard_map/all_to_all | solution.py:20
  286.8 37.3 %all-to-all-start.6 = ((bf16[64,32,256]{2,1,0:T(8,128)(2,1)}), bf16[64,32,256]{2,1,0:T(8,128)(2,1)S(1)}, u32[]{:S(2)}, u32[]{:S(2)}) async-start(bf16[64,32,256]{2,1,0:T(8,128)(2,1)} %broadcast_in_dim.64), calls=%async_computation.6 | async-start | bytes 2097152 | tf_op jit(solution)/shard_map/all_to_all | solution.py:20
  325.6 34.5 %all-to-all-start.7 = ((bf16[64,32,256]{2,1,0:T(8,128)(2,1)}), bf16[64,32,256]{2,1,0:T(8,128)(2,1)S(1)}, u32[]{:S(2)}, u32[]{:S(2)}) async-start(bf16[64,32,256]{2,1,0:T(8,128)(2,1)} %broadcast_in_dim.65), calls=%async_computation.7 | async-start | bytes 2097152 | tf_op jit(solution)/shard_map/all_to_all | solution.py:20
where the time goes:
time: 363 us; the launch traced here: 361 us
  blocking collectives  192 us (53%)
  waiting for transfers between devices  112 us (31%)
  starting transfers between devices  34.5 us (10%)
  matrix products  15 us (4%)
  local copies, waits for them, and re-layouts  7.06 us (2%)
    all_to_all x4, waiting for transfers between devices, copy_for_each(): lax.all_to_all(jnp.broadcast_to(x[None], (length, *x.shape)), axis, 0, 0,...  112 us
    all_to_all x3, blocking collectives, copy_for_each(): lax.all_to_all(jnp.broadcast_to(x[None], (length, *x.shape)), axis, 0, 0,...  103 us
    all_to_all x1, blocking collectives, sent_and_summed(): pieces = lax.all_to_all(cut_along(x, dim, length), axis, 0, 0, tiled=True)  61.8 us
    all_to_all x4, starting transfers between devices, copy_for_each(): lax.all_to_all(jnp.broadcast_to(x[None], (length, *x.shape)), axis, 0, 0,...  34.5 us
    all_gather x3, blocking collectives, from_root(): lax.all_gather(x, axis)  26.9 us
    dot_general x8, matrix products, local(): jnp.dot(coded, earlier, preferred_element_type=jnp.float32)  12.4 us
  transfers between devices with their start and end apart: 4, of which 4 were waited for; matrix products, arithmetic and copies ran while one was open for 0% of the time, Pallas kernels for 0%

commit v1 on v0

v1 whole, which is shorter than its diff:
```python
import functools

import jax
import jax.numpy as jnp
from jax import lax
from jax.experimental import pallas as pl
from jax.experimental.pallas import tpu as pltpu
from jax.sharding import PartitionSpec as P

MESH = pl.DeviceIdType.MESH
F32, BF16 = jnp.float32, jnp.bfloat16


def dot_t(a, b):
    return lax.dot_general(a, b, (((1,), (1,)), ((), ())), preferred_element_type=F32)


def kernel(
    np_, nz, ny,
    right_ref, prior_ref, codes_ref, scale_ref, diag_ref, inner_ref, out_ref,
    right_v, prior_v, codes_v, prior_t, place, pt, core_out, core_in, half_sum, y_out, y_in, z_out, z_in,
    w, act, x_out, res, final_out, final_in,
    in_sem, codes_sem, w_sem, wy_s, wy_r, wc_s, wc_r, c_s, c_r, y_s, y_r, z_s, z_r, a_s, a_r, x_s, f_s, f_r,
):
    p, j = lax.axis_index("row"), lax.axis_index("col")
    group = ny * 2
    z, g = j // group, j % group
    y, c = g // 2, g % 2
    rows = right_ref.shape[0]
    blocks = scale_ref.shape[1]
    kb = prior_ref.shape[0] // blocks
    row_block = rows * group
    half = right_ref.shape[1] // 2
    chunk = half // ny

    def col_of(z_, y_, c_):
        return z_ * group + y_ * 2 + c_

    def remote(src, dst, send, recv, row, col):
        return pltpu.make_async_remote_copy(
            src_ref=src, dst_ref=dst, send_sem=send, recv_sem=recv, device_id={"row": row, "col": col}, device_id_type=MESH
        )

    barrier = pltpu.get_barrier_semaphore()

    def greet(row, col):
        pl.semaphore_signal(barrier, inc=1, device_id={"row": row, "col": col}, device_id_type=MESH)

    greet(p, col_of(z, y, 1 - c))

    @pl.loop(1, ny)
    def _(d):
        greet(p, col_of(z, (y + d) % ny, c))
        greet(p, col_of(z, (y + d) % ny, 1 - c))

    @pl.loop(1, nz)
    def _(d):
        greet(p, col_of((z + d) % nz, y, c))

    @pl.loop(1, np_)
    def _(d):
        @pl.loop(0, nz)
        def _(zz):
            greet((p + d) % np_, col_of(zz, y, c))

    load_prior = pltpu.make_async_copy(prior_ref, prior_v, in_sem.at[0])
    load_right = pltpu.make_async_copy(right_ref, right_v, in_sem.at[1])
    load_prior.start()
    load_right.start()

    def load_codes(i):
        zb = (z + 1 + i) % nz
        return pltpu.make_async_copy(
            codes_ref.at[pl.ds(pl.multiple_of(zb * row_block, row_block), row_block)], codes_v.at[i], codes_sem.at[i]
        )

    @pl.loop(0, nz)
    def _(i):
        load_codes(i).start()

    def load_inner(m):
        return pltpu.make_async_copy(inner_ref.at[0, m], w.at[m, g], w_sem.at[m])

    load_diag = pltpu.make_async_copy(diag_ref.at[0], w.at[p, g], w_sem.at[p])

    @pl.loop(0, p)
    def _(m):
        load_inner(m).start()

    load_diag.start()

    load_prior.wait()
    for b in range(blocks):
        part = prior_v[b * kb : (b + 1) * kb, :].astype(F32) * scale_ref[0, b]
        prior_t[:, b * kb : (b + 1) * kb] = part.T.astype(BF16)
    load_right.wait()
    place[...] = jnp.zeros_like(place)
    place[pl.ds(pl.multiple_of(g * rows, rows), rows), :] = right_v[...]

    pl.semaphore_wait(barrier, 1 + 2 * (ny - 1) + (nz - 1) + (np_ - 1) * nz)

    def w_y(m, d):
        to = (y + d) % ny
        return remote(w.at[m, g], w.at[m, g], wy_s.at[m, d], wy_r.at[m, y], p, col_of(z, to, c))

    def w_y_arrival(m, d):
        src = (y + d) % ny
        slot = src * 2 + c
        return remote(w.at[m, slot], w.at[m, slot], wy_s.at[m, d], wy_r.at[m, src], p, col_of(z, src, c))

    def w_c(m, yy):
        slot = yy * 2 + c
        return remote(w.at[m, slot], w.at[m, slot], wc_s.at[m, yy], wc_r.at[m, yy], p, col_of(z, y, 1 - c))

    def w_c_arrival(m, yy):
        slot = yy * 2 + 1 - c
        return remote(w.at[m, slot], w.at[m, slot], wc_s.at[m, yy], wc_r.at[m, yy], p, col_of(z, y, 1 - c))

    load_diag.wait()

    @pl.loop(0, p)
    def _(m):
        load_inner(m).wait()

    @pl.loop(0, p + 1)
    def _(m):
        @pl.loop(1, ny)
        def _(d):
            w_y(m, d).start()

        w_c(m, y).start()

    def forward(m):
        @pl.loop(1, ny)
        def _(d):
            w_y_arrival(m, d).wait_recv()
            w_c(m, (y + d) % ny).start()

    def core_copy(i):
        return remote(core_out.at[i], core_in.at[i], c_s.at[i], c_r.at[i], p, col_of(z, y, 1 - c))

    def y_copy(i, d):
        to = (y + d) % ny
        return remote(y_out.at[i, to], y_in.at[i, y], y_s.at[i, d], y_r.at[i, y], p, col_of(z, to, c))

    def y_arrival(i, d):
        src = (y + d) % ny
        return remote(y_out.at[i, src], y_in.at[i, src], y_s.at[i, d], y_r.at[i, src], p, col_of(z, src, c))

    def z_copy(i):
        to = (z + 1 + i) % nz
        return remote(z_out.at[i], z_in.at[z], z_s.at[i], z_r.at[z], p, col_of(to, y, c))

    def z_arrival(d):
        src = (z + d) % nz
        return remote(z_out.at[0], z_in.at[src], z_s.at[0], z_r.at[src], p, col_of(src, y, c))

    def across_y(i):
        core_copy(i).wait_recv()
        total = half_sum[i].reshape(half, row_block) + core_in[i].astype(F32)
        total = total.reshape(ny, chunk, row_block)
        half_sum[i] = total
        y_out[i] = total.astype(BF16)

        @pl.loop(1, ny)
        def _(d):
            y_copy(i, d).start()

    def across_z(i):
        total = half_sum[i, y]
        for d in range(1, ny):
            y_arrival(i, d).wait_recv()
            total = total + y_in[i, (y + d) % ny].astype(F32)
        return total

    lag = min(2, nz - 1)

    @pl.loop(0, nz)
    def _(i):
        load_codes(i).wait()
        pt[...] = dot_t(prior_t[...], codes_v[i]).reshape(2, half, row_block)

        @pl.when(i == nz - 1)
        def _():
            pt[...] -= place[...].T.reshape(2, half, row_block)

        core_out[i] = pt[1 - c].astype(BF16)
        core_copy(i).start()
        half_sum[i] = pt[c].reshape(ny, chunk, row_block)

        @pl.when(i >= lag)
        def _():
            across_y(i - lag)

    @pl.loop(nz - lag, nz)
    def _(i):
        across_y(i)

    forward(0)

    @pl.loop(0, nz - 1)
    def _(i):
        z_out[i] = across_z(i).astype(BF16)
        z_copy(i).start()

    own = across_z(nz - 1)
    for d in range(1, nz):
        z_arrival(d).wait_recv()
        own = own + z_in[(z + d) % nz].astype(F32)
    res[...] = -own

    def times(s, skip_own):
        @pl.loop(0, ny)
        def _(yy):
            w_c_arrival(s, yy).wait_recv()

        total = jnp.zeros((chunk, row_block), F32)
        for d in range(nz):
            src = (z + d) % nz
            if not (skip_own and d == 0):
                remote(x_out, act.at[s, src], x_s.at[0, 0], a_r.at[s, src], p, col_of(src, y, c)).wait_recv()
            columns = pl.ds(pl.multiple_of(src * row_block, row_block), row_block)
            total = total + dot_t(act[s, src], w[s, :, :, columns].reshape(row_block, row_block))
        return total

    @pl.loop(0, p)
    def _(s):
        forward(s + 1)
        res[...] -= times(s, False)

    act[p, z] = res[...].astype(BF16)

    def a_copy(d):
        to = (z + d) % nz
        return remote(act.at[p, z], act.at[p, z], a_s.at[d], a_r.at[p, z], p, col_of(to, y, c))

    @pl.loop(1, nz)
    def _(d):
        a_copy(d).start()

    solved = times(p, True)
    x_out[...] = solved.astype(BF16)

    def x_copy(q, d):
        to = (z + d) % nz
        return remote(x_out, act.at[p, z], x_s.at[q, d], a_r.at[p, z], q, col_of(to, y, c))

    @pl.loop(p + 1, np_)
    def _(q):
        @pl.loop(0, nz)
        def _(d):
            x_copy(q, d).start()

    place[:half, :row_block] = jnp.zeros((half, row_block), F32)
    place[pl.ds(pl.multiple_of(y * chunk, chunk), chunk), :row_block] = solved
    final_out[...] = place[:half, :row_block].T.reshape(group, rows, half)

    def f_copy(d):
        to = (g + d) % group
        return remote(final_out.at[to], final_in.at[g], f_s.at[d], f_r.at[g], p, z * group + to)

    def f_arrival(d):
        src = (g + d) % group
        return remote(final_out.at[src], final_in.at[src], f_s.at[d], f_r.at[src], p, z * group + src)

    @pl.loop(1, group)
    def _(d):
        f_copy(d).start()

    final_in[g] = final_out[g]

    @pl.loop(1, group)
    def _(d):
        f_arrival(d).wait_recv()

    for cc in range(2):
        total = final_in[cc]
        for yy in range(1, ny):
            total = total + final_in[yy * 2 + cc]
        out_ref[:, cc * half : (cc + 1) * half] = total

    @pl.loop(0, p + 1)
    def _(m):
        @pl.loop(1, ny)
        def _(d):
            w_y(m, d).wait_send()

        @pl.loop(0, ny)
        def _(yy):
            w_c(m, yy).wait_send()

    @pl.loop(0, nz)
    def _(i):
        core_copy(i).wait_send()

        @pl.loop(1, ny)
        def _(d):
            y_copy(i, d).wait_send()

    @pl.loop(0, nz - 1)
    def _(i):
        z_copy(i).wait_send()
        a_copy(i + 1).wait_send()

    @pl.loop(p + 1, np_)
    def _(q):
        @pl.loop(0, nz)
        def _(d):
            x_copy(q, d).wait_send()

    @pl.loop(1, group)
    def _(d):
        f_copy(d).wait_send()


def local(np_, nz, ny, right_side, prior_solution, factor_codes, block_scale, diag_inverse, inner_factor):
    rows, rhs = right_side.shape
    depth = prior_solution.shape[0]
    group = ny * 2
    row_block = rows * group
    half = rhs // 2
    chunk = half // ny
    width = diag_inverse.shape[-1]
    dma = pltpu.SemaphoreType.DMA
    scratch = [
        pltpu.VMEM((rows, rhs), F32),
        pltpu.VMEM((depth, rhs), BF16),
        pltpu.VMEM((nz, row_block, depth), BF16),
        pltpu.VMEM((rhs, depth), BF16),
        pltpu.VMEM((row_block, rhs), F32),
        pltpu.VMEM((2, half, row_block), F32),
        pltpu.VMEM((nz, half, row_block), BF16),
        pltpu.VMEM((nz, half, row_block), BF16),
        pltpu.VMEM((nz, ny, chunk, row_block), F32),
        pltpu.VMEM((nz, ny, chunk, row_block), BF16),
        pltpu.VMEM((nz, ny, chunk, row_block), BF16),
        pltpu.VMEM((nz, chunk, row_block), BF16),
        pltpu.VMEM((nz, chunk, row_block), BF16),
        pltpu.VMEM((np_, group, rows, width), BF16),
        pltpu.VMEM((np_, nz, chunk, row_block), BF16),
        pltpu.VMEM((chunk, row_block), BF16),
        pltpu.VMEM((chunk, row_block), F32),
        pltpu.VMEM((group, rows, half), F32),
        pltpu.VMEM((group, rows, half), F32),
        dma((2,)),
        dma((nz,)),
        dma((np_,)),
        dma((np_, ny)),
        dma((np_, ny)),
        dma((np_, ny)),
        dma((np_, ny)),
        dma((nz,)),
        dma((nz,)),
        dma((nz, ny)),
        dma((nz, ny)),
        dma((nz,)),
        dma((nz,)),
        dma((nz,)),
        dma((np_, nz)),
        dma((np_, nz)),
        dma((group,)),
        dma((group,)),
    ]
    anywhere = pl.BlockSpec(memory_space=pl.ANY)
    return pl.pallas_call(
        functools.partial(kernel, np_, nz, ny),
        out_shape=jax.ShapeDtypeStruct((rows, rhs), F32),
        in_specs=[anywhere, anywhere, anywhere, pl.BlockSpec(memory_space=pltpu.SMEM), anywhere, anywhere],
        out_specs=pl.BlockSpec(memory_space=pltpu.VMEM),
        scratch_shapes=scratch,
        compiler_params=pltpu.CompilerParams(collective_id=0, has_side_effects=True, vmem_limit_bytes=48 * 2**20),
        cost_estimate=pl.CostEstimate(
            flops=2 * nz * row_block * depth * rhs, bytes_accessed=2 * nz * row_block * depth, transcendentals=0
        ),
    )(right_side, prior_solution, factor_codes, block_scale, diag_inverse, inner_factor)


def build(mesh, ny):
    np_ = mesh.shape["row"]
    nz = mesh.shape["col"] // (2 * ny)
    return jax.shard_map(
        functools.partial(local, np_, nz, ny),
        mesh=mesh,
        in_specs=(
            P(("row", "col"), None),
            P("col", None),
            P("row", "col"),
            P("row", "col"),
            P("row", "col", None),
            P("row", None, "col", None),
        ),
        out_specs=P(("row", "col"), None),
        check_vma=False,
    )


def solution(mesh):
    return build(mesh, 4)
```

time: 363 us -> 86.4 us (0.24)
  blocking collectives: 192 us -> 0 us
  waiting for transfers between devices: 112 us -> 0 us
  Pallas kernels: 0 us -> 80.9 us
  starting transfers between devices: 34.5 us -> 0 us
  matrix products: 15 us -> 0 us
    all_to_all x4 -> x0, blocking collectives: 165 us -> none  [the longest x3 103 us: copy_for_each(): lax.all_to_all(jnp.broadcast_to(x[None], (length, *x.shape)), axis, 0, 0,...]
    all_to_all x4 -> x0, waiting for transfers between devices: 112 us -> none  [copy_for_each(): lax.all_to_all(jnp.broadcast_to(x[None], (length, *x.shape)), axis, 0, 0,...]
    pallas_call x0 -> x1, Pallas kernels: none -> 80.9 us  [local(): pl.pallas_call(functools.partial(kernel, np_, nz, ny), out_shape=jax.Shap...]
    all_to_all x4 -> x0, starting transfers between devices: 34.5 us -> none  [copy_for_each(): lax.all_to_all(jnp.broadcast_to(x[None], (length, *x.shape)), axis, 0, 0,...]
    all_gather x3 -> x0, blocking collectives: 26.9 us -> none  [from_root(): lax.all_gather(x, axis)]
    dot_general x15 -> x0, matrix products: 15 us -> none  [the longest x8 12.4 us: local(): jnp.dot(coded, earlier, preferred_element_type=jnp.float32)]
    broadcast_in_dim x7 -> x0, local copies, waits for them, and re-layouts: 4.8 us -> none  [copy_for_each(): jnp.broadcast_to(x[None], (length, *x.shape))]
    unnamed x10 -> x11, local copies, waits for them, and re-layouts: 0.64 us -> 5.2 us
  transfers between devices with their start and end apart: 4 -> 0, of which waited for: 4 -> 0; matrix products, arithmetic and copies ran while one was open for 0% -> 0% of each run, Pallas kernels for 0% -> 0%
where the time goes in v1:
time: 86.4 us; the launch traced here: 86.1 us
  Pallas kernels  80.9 us (94%)
  local copies, waits for them, and re-layouts  5.2 us (6%)
    pallas_call x1, Pallas kernels, local(): pl.pallas_call(functools.partial(kernel, np_, nz, ny), out_shape=jax.Shap...  80.9 us
    unnamed x11, local copies, waits for them, and re-layouts  5.2 us

profile of v1, /device:TPU:7, one launch (start us, length us, event | category | flops | bytes accessed | tf_op | source)
XLA Modules:
  0.0 86.1 jit_solution(17645493484009418856)
XLA Ops:
  0.0 0.0 copy-start
  0.0 1.2 %copy-done = bf16[2048,256]{1,0:T(8,128)(2,1)S(1)} copy-done((bf16[2048,256]{1,0:T(8,128)(2,1)S(1)}, bf16[2048,256]{1,0:T(8,128)(2,1)}, u32[]{:S(2)}) %copy-start) | copy-done | bytes 1048600
  1.2 0.0 copy-start.1
  1.2 1.0 %copy-done.1 = bf16[1,4,32,2048]{3,2,1,0:T(8,128)(2,1)S(1)} copy-done((bf16[1,4,32,2048]{3,2,1,0:T(8,128)(2,1)S(1)}, bf16[1,4,32,2048]{3,2,1,0:T(8,128)(2,1)}, u32[]{:S(2)}) %copy-start.1) | copy-done | bytes 524312
  2.3 0.0 copy-start.2
  2.3 0.9 %copy-done.2 = bf16[1,32,2048]{2,1,0:T(8,128)(2,1)S(1)} copy-done((bf16[1,32,2048]{2,1,0:T(8,128)(2,1)S(1)}, bf16[1,32,2048]{2,1,0:T(8,128)(2,1)}, u32[]{:S(2)}) %copy-start.2) | copy-done | bytes 131096
  3.2 0.0 copy-start.3
  3.2 0.8 copy-done.3
  3.9 0.0 copy-start.4
  3.9 0.7 copy-done.4
  4.6 80.9 %shard_map.64 = f32[32,256]{1,0:T(8,128)S(1)} custom-call(f32[32,256]{1,0:T(8,128)S(1)} %copy-done.3, bf16[2048,256]{1,0:T(8,128)(2,1)S(1)} %copy-done, bf16[2048,2048]{1,0:T(8,128)(2,1)} %codes_ref.1, f32[1,8]{1,0:T(1,128)S(1)} %copy-done.4, bf16[1,32,2048]{2,1,0:T(8,128)(2,1)S(1)} %copy-done.2, bf16[1,4,32,2048]{3,2,1,0:T(8,128)(2,1)S(1)} %copy-done.1), custom_call_target="tpu_custom_call" | custom-call | flops 2147483648 | bytes 8388608 | tf_op jit(solution)/shard_map/pallas_call | solution.py:365
  85.5 0.6 copy.8
Async XLA Ops:
  0.0 1.2 %copy-start = (bf16[2048,256]{1,0:T(8,128)(2,1)S(1)}, bf16[2048,256]{1,0:T(8,128)(2,1)}, u32[]{:S(2)}) copy-start(bf16[2048,256]{1,0:T(8,128)(2,1)} %prior_ref.1) | copy-start | bytes 3145732
  1.2 1.0 %copy-start.1 = (bf16[1,4,32,2048]{3,2,1,0:T(8,128)(2,1)S(1)}, bf16[1,4,32,2048]{3,2,1,0:T(8,128)(2,1)}, u32[]{:S(2)}) copy-start(bf16[1,4,32,2048]{3,2,1,0:T(8,128)(2,1)} %inner_ref.1) | copy-start | bytes 1572868
  2.3 0.9 %copy-start.2 = (bf16[1,32,2048]{2,1,0:T(8,128)(2,1)S(1)}, bf16[1,32,2048]{2,1,0:T(8,128)(2,1)}, u32[]{:S(2)}) copy-start(bf16[1,32,2048]{2,1,0:T(8,128)(2,1)} %diag_ref.1) | copy-start | bytes 393220
  3.2 0.8 copy-start.3
  3.9 0.7 copy-start.4

commit v2 on v1

--- a/solution.py
+++ b/solution.py
@@ -19,8 +19,8 @@
     np_, nz, ny,
     right_ref, prior_ref, codes_ref, scale_ref, diag_ref, inner_ref, out_ref,
     right_v, prior_v, codes_v, prior_t, place, pt, core_out, core_in, half_sum, y_out, y_in, z_out, z_in,
-    w, act, x_out, res, final_out, final_in,
-    in_sem, codes_sem, w_sem, wy_s, wy_r, wc_s, wc_r, c_s, c_r, y_s, y_r, z_s, z_r, a_s, a_r, x_s, f_s, f_r,
+    w, lcol, macc, mw, act, x_out, res, final_out, final_in,
+    in_sem, codes_sem, w_sem, wy_s, wy_r, wc_s, wc_r, la_s, la_r, l_s, l_r, my_s, my_r, mc_s, mc_r, c_s, c_r, y_s, y_r, z_s, z_r, a_s, a_r, x_s, f_s, f_r,
 ):
     p, j = lax.axis_index("row"), lax.axis_index("col")
     group = ny * 2
@@ -32,6 +32,8 @@
     row_block = rows * group
     half = right_ref.shape[1] // 2
     chunk = half // ny
+    last = jnp.maximum(p - 1, 0)
+    far_first = sorted(range(nz), key=lambda d: -min(d, nz - d))
 
     def col_of(z_, y_, c_):
         return z_ * group + y_ * 2 + c_
@@ -122,19 +124,92 @@
     def _(m):
         load_inner(m).wait()
 
-    @pl.loop(0, p + 1)
-    def _(m):
+    def share(m):
         @pl.loop(1, ny)
         def _(d):
             w_y(m, d).start()
 
         w_c(m, y).start()
+
+    def gathered(m):
+        @pl.loop(0, ny)
+        def _(yy):
+            w_c_arrival(m, yy).wait_recv()
 
     def forward(m):
         @pl.loop(1, ny)
         def _(d):
             w_y_arrival(m, d).wait_recv()
             w_c(m, (y + d) % ny).start()
+
+    own_columns = pl.ds(pl.multiple_of(g * row_block, row_block), row_block)
+
+    def la_copy(d):
+        to = (g + d) % group
+        columns = pl.ds(pl.multiple_of(to * row_block, row_block), row_block)
+        return remote(w.at[last, g, :, columns], lcol.at[z, g], la_s.at[d], la_r.at[g], p, z * group + to)
+
+    def la_arrival(d):
+        src = (g + d) % group
+        return remote(lcol.at[z, src], lcol.at[z, src], la_s.at[d], la_r.at[src], p, z * group + src)
+
+    far = nz // 2
+
+    def l_half(owner, h):
+        return lcol.at[owner, pl.ds(pl.multiple_of(h * (group // 2), group // 2), group // 2)]
+
+    def l_move(k, h, way):
+        step = 1 - 2 * way
+        owner = (z + nz - (k - 1) * step) % nz
+        to = (z + nz + step) % nz
+        part = l_half(owner, h)
+        return remote(part, part, l_s.at[way, k - 1, h], l_r.at[owner, h], p, col_of(to, y, c))
+
+    def l_arrival(off, h):
+        owner = (z + off) % nz
+        part = l_half(owner, h)
+        return remote(part, part, l_s.at[0, 0, h], l_r.at[owner, h], p, col_of((z + 1) % nz, y, c))
+
+    def l_start(h):
+        l_move(1, h, 0).start()
+        if far > 1:
+            l_move(1, h, 1).start()
+
+    def l_pass(k, h):
+        l_arrival(nz - k, h).wait_recv()
+        l_move(k + 1, h, 0).start()
+
+        @pl.when(k < far - 1)
+        def _():
+            l_arrival(k, h).wait_recv()
+            l_move(k + 1, h, 1).start()
+
+    @pl.when(p > 0)
+    def _():
+        @pl.loop(1, group)
+        def _(d):
+            la_copy(d).start()
+
+        lcol[z, g] = w[last, g, :, own_columns]
+
+    share(p)
+
+    def m_y(d):
+        to = (y + d) % ny
+        return remote(mw.at[g], mw.at[g], my_s.at[d], my_r.at[y], p, col_of(z, to, c))
+
+    def m_y_arrival(d):
+        src = (y + d) % ny
+        slot = src * 2 + c
+        return remote(mw.at[slot], mw.at[slot], my_s.at[d], my_r.at[src], p, col_of(z, src, c))
+
+    def m_c(yy):
+        slot = yy * 2 + c
+        return remote(mw.at[slot], mw.at[slot], mc_s.at[yy], mc_r.at[yy], p, col_of(z, y, 1 - c))
+
+    def m_c_arrival(yy):
+        slot = yy * 2 + 1 - c
+        return remote(mw.at[slot], mw.at[slot], mc_s.at[yy], mc_r.at[yy], p, col_of(z, y, 1 - c))
 
     def core_copy(i):
         return remote(core_out.at[i], core_in.at[i], c_s.at[i], c_r.at[i], p, col_of(z, y, 1 - c))
@@ -192,16 +267,40 @@
         def _():
             across_y(i - lag)
 
+        @pl.when((i == nz // 2) & (p > 0))
+        def _():
+            @pl.loop(1, group)
+            def _(d):
+                la_arrival(d).wait_recv()
+
+            @pl.loop(0, 2)
+            def _(h):
+                l_start(h)
+
     @pl.loop(nz - lag, nz)
     def _(i):
         across_y(i)
 
-    forward(0)
+    @pl.loop(0, p - 1)
+    def _(m):
+        share(m)
+
+    @pl.when(p == 0)
+    def _():
+        forward(p)
 
     @pl.loop(0, nz - 1)
     def _(i):
         z_out[i] = across_z(i).astype(BF16)
         z_copy(i).start()
+
+        @pl.when((p > 0) & (i < 2 * far - 2))
+        def _():
+            l_pass(1 + i // 2, i % 2)
+
+    @pl.when(p > 0)
+    def _():
+        forward(p)
 
     own = across_z(nz - 1)
     for d in range(1, nz):
@@ -209,36 +308,106 @@
         own = own + z_in[(z + d) % nz].astype(F32)
     res[...] = -own
 
-    def times(s, skip_own):
-        @pl.loop(0, ny)
-        def _(yy):
-            w_c_arrival(s, yy).wait_recv()
-
+    def a_copy(d):
+        to = (z + d) % nz
+        return remote(act.at[p, z], act.at[p, z], a_s.at[d], a_r.at[p, z], p, col_of(to, y, c))
+
+    def send_current():
+        act[p, z] = res[...].astype(BF16)
+
+        for d in far_first[:-1]:
+            a_copy(d).start()
+
+    def act_arrival(s, src):
+        return remote(x_out, act.at[s, src], x_s.at[0, 0], a_r.at[s, src], p, col_of(src, y, c))
+
+    def times(s, own_here):
         total = jnp.zeros((chunk, row_block), F32)
         for d in range(nz):
             src = (z + d) % nz
-            if not (skip_own and d == 0):
-                remote(x_out, act.at[s, src], x_s.at[0, 0], a_r.at[s, src], p, col_of(src, y, c)).wait_recv()
+            if not (own_here and d == 0):
+                act_arrival(s, src).wait_recv()
             columns = pl.ds(pl.multiple_of(src * row_block, row_block), row_block)
             total = total + dot_t(act[s, src], w[s, :, :, columns].reshape(row_block, row_block))
         return total
 
-    @pl.loop(0, p)
-    def _(s):
-        forward(s + 1)
-        res[...] -= times(s, False)
-
-    act[p, z] = res[...].astype(BF16)
-
-    def a_copy(d):
-        to = (z + d) % nz
-        return remote(act.at[p, z], act.at[p, z], a_s.at[d], a_r.at[p, z], p, col_of(to, y, c))
-
-    @pl.loop(1, nz)
-    def _(d):
-        a_copy(d).start()
-
-    solved = times(p, True)
+    @pl.when(p <= 1)
+    def _():
+        send_current()
+
+    @pl.when(p > 0)
+    def _():
+        gathered(p)
+
+        @pl.loop(0, p - 1)
+        def _(m):
+            forward(m)
+
+        def columns_of(d):
+            return pl.ds(pl.multiple_of(((z + d) % nz) * row_block, row_block), row_block)
+
+        def part(d, block):
+            return jnp.dot(
+                w[p, :, :, columns_of(d)].reshape(row_block, row_block),
+                block.reshape(row_block, row_block),
+                preferred_element_type=F32,
+            )
+
+        macc[...] = jnp.zeros_like(macc)
+
+        @pl.loop(1, nz + 1)
+        def _(t):
+            off = (t + far) % nz
+
+            @pl.when((off == far) | ((off == far - 1) & (off > 0)))
+            def _():
+                @pl.loop(0, 2)
+                def _(h):
+                    l_arrival(off, h).wait_recv()
+
+            macc[...] += part(off, lcol[(z + off) % nz])
+
+        mw[g] = macc[...].astype(BF16)
+
+        @pl.loop(1, ny)
+        def _(d):
+            m_y(d).start()
+
+        m_c(y).start()
+
+        @pl.loop(1, ny)
+        def _(d):
+            m_y_arrival(d).wait_recv()
+            m_c((y + d) % ny).start()
+
+        @pl.loop(0, p - 1)
+        def _(s):
+            gathered(s)
+            res[...] -= times(s, False)
+
+    @pl.when(p > 1)
+    def _():
+        send_current()
+
+    @pl.when(p == 0)
+    def _():
+        gathered(p)
+
+    res[...] = times(p, True)
+
+    @pl.when(p > 0)
+    def _():
+        @pl.loop(0, ny)
+        def _(yy):
+            m_c_arrival(yy).wait_recv()
+
+        total = jnp.zeros((chunk, row_block), F32)
+        for src in range(nz):
+            act_arrival(last, src).wait_recv()
+            total = total + dot_t(act[last, src], mw[src])
+        res[...] -= total
+
+    solved = res[...]
     x_out[...] = solved.astype(BF16)
 
     def x_copy(q, d):
@@ -247,8 +416,7 @@
 
     @pl.loop(p + 1, np_)
     def _(q):
-        @pl.loop(0, nz)
-        def _(d):
+        for d in far_first:
             x_copy(q, d).start()
 
     place[:half, :row_block] = jnp.zeros((half, row_block), F32)
@@ -279,8 +447,7 @@
             total = total + final_in[yy * 2 + cc]
         out_ref[:, cc * half : (cc + 1) * half] = total
 
-    @pl.loop(0, p + 1)
-    def _(m):
+    def shared(m):
         @pl.loop(1, ny)
         def _(d):
             w_y(m, d).wait_send()
@@ -288,6 +455,36 @@
         @pl.loop(0, ny)
         def _(yy):
             w_c(m, yy).wait_send()
+
+    shared(p)
+
+    @pl.loop(0, p - 1)
+    def _(m):
+        shared(m)
+
+    @pl.when(p > 0)
+    def _():
+        @pl.loop(1, group)
+        def _(d):
+            la_copy(d).wait_send()
+
+        @pl.loop(0, 2)
+        def _(h):
+            @pl.loop(1, far + 1)
+            def _(k):
+                l_move(k, h, 0).wait_send()
+
+            @pl.loop(1, far)
+            def _(k):
+                l_move(k, h, 1).wait_send()
+
+        @pl.loop(1, ny)
+        def _(d):
+            m_y(d).wait_send()
+
+        @pl.loop(0, ny)
+        def _(yy):
+            m_c(yy).wait_send()
 
     @pl.loop(0, nz)
     def _(i):
@@ -337,6 +534,9 @@
         pltpu.VMEM((nz, chunk, row_block), BF16),
         pltpu.VMEM((nz, chunk, row_block), BF16),
         pltpu.VMEM((np_, group, rows, width), BF16),
+        pltpu.VMEM((nz, group, rows, row_block), BF16),
+        pltpu.VMEM((row_block, row_block), F32),
+        pltpu.VMEM((group, row_block, row_block), BF16),
         pltpu.VMEM((np_, nz, chunk, row_block), BF16),
         pltpu.VMEM((chunk, row_block), BF16),
         pltpu.VMEM((chunk, row_block), F32),
@@ -349,6 +549,14 @@
         dma((np_, ny)),
         dma((np_, ny)),
         dma((np_, ny)),
+        dma((group,)),
+        dma((group,)),
+        dma((2, nz // 2, 2)),
+        dma((nz, 2)),
+        dma((ny,)),
+        dma((ny,)),
+        dma((ny,)),
+        dma((ny,)),
         dma((nz,)),
         dma((nz,)),
         dma((nz, ny)),
@@ -368,7 +576,7 @@
         in_specs=[anywhere, anywhere, anywhere, pl.BlockSpec(memory_space=pltpu.SMEM), anywhere, anywhere],
         out_specs=pl.BlockSpec(memory_space=pltpu.VMEM),
         scratch_shapes=scratch,
-        compiler_params=pltpu.CompilerParams(collective_id=0, has_side_effects=True, vmem_limit_bytes=48 * 2**20),
+        compiler_params=pltpu.CompilerParams(collective_id=0, has_side_effects=True, vmem_limit_bytes=60 * 2**20),
         cost_estimate=pl.CostEstimate(
             flops=2 * nz * row_block * depth * rhs, bytes_accessed=2 * nz * row_block * depth, transcendentals=0
         ),

time: 86.4 us -> 72.7 us (0.84)
  Pallas kernels: 80.9 us -> 71.1 us
  local copies, waits for them, and re-layouts: 5.2 us -> 1.38 us
    pallas_call x1, Pallas kernels: 80.9 us -> 71.1 us  [local(): pl.pallas_call(functools.partial(kernel, np_, nz, ny), out_shape=jax.Shap...]
    unnamed x11 -> x1, local copies, waits for them, and re-layouts: 5.2 us -> 1.38 us
where the time goes in v2:
time: 72.7 us; the launch traced here: 72.5 us
  Pallas kernels  71.1 us (98%)
  local copies, waits for them, and re-layouts  1.38 us (2%)
    pallas_call x1, Pallas kernels, local(): pl.pallas_call(functools.partial(kernel, np_, nz, ny), out_shape=jax.Shap...  71.1 us

profile of v2, /device:TPU:7, one launch (start us, length us, event | category | flops | bytes accessed | tf_op | source)
XLA Modules:
  0.0 72.5 jit_solution(1259969668536099124)
XLA Ops:
  0.0 71.1 %shard_map.64 = f32[32,256]{1,0:T(8,128)} custom-call(f32[32,256]{1,0:T(8,128)} %right_ref.1, bf16[2048,256]{1,0:T(8,128)(2,1)} %prior_ref.1, bf16[2048,2048]{1,0:T(8,128)(2,1)} %codes_ref.1, f32[1,8]{1,0:T(1,128)} %scale_ref.1, bf16[1,32,2048]{2,1,0:T(8,128)(2,1)} %diag_ref.1, bf16[1,4,32,2048]{3,2,1,0:T(8,128)(2,1)} %inner_ref.1), custom_call_target="tpu_custom_call" | custom-call | flops 2147483648 | bytes 8388608 | tf_op jit(solution)/shard_map/pallas_call | solution.py:573
  71.2 1.4 %copy.8 = f32[32,256]{1,0:T(8,128)} copy(f32[32,256]{1,0:T(8,128)} %shard_map.64) | data formatting | bytes 65536

commit v3 on v2

--- a/solution.py
+++ b/solution.py
@@ -20,7 +20,7 @@
     right_ref, prior_ref, codes_ref, scale_ref, diag_ref, inner_ref, out_ref,
     right_v, prior_v, codes_v, prior_t, place, pt, core_out, core_in, half_sum, y_out, y_in, z_out, z_in,
     w, lcol, macc, mw, act, x_out, res, final_out, final_in,
-    in_sem, codes_sem, w_sem, wy_s, wy_r, wc_s, wc_r, la_s, la_r, l_s, l_r, my_s, my_r, mc_s, mc_r, c_s, c_r, y_s, y_r, z_s, z_r, a_s, a_r, x_s, f_s, f_r,
+    in_sem, codes_sem, w_sem, wy_s, wy_r, wc_s, wc_r, la_s, la_r, l_s, l_r, my_s, my_r, mc_s, mc_r, c_s, c_r, y_s, y_r, z_s, z_r, a_s, a_r, x_s, f_s, f_r, ready,
 ):
     p, j = lax.axis_index("row"), lax.axis_index("col")
     group = ny * 2
@@ -61,9 +61,7 @@
 
     @pl.loop(1, np_)
     def _(d):
-        @pl.loop(0, nz)
-        def _(zz):
-            greet((p + d) % np_, col_of(zz, y, c))
+        greet((p + d) % np_, j)
 
     load_prior = pltpu.make_async_copy(prior_ref, prior_v, in_sem.at[0])
     load_right = pltpu.make_async_copy(right_ref, right_v, in_sem.at[1])
@@ -99,7 +97,11 @@
     place[...] = jnp.zeros_like(place)
     place[pl.ds(pl.multiple_of(g * rows, rows), rows), :] = right_v[...]
 
-    pl.semaphore_wait(barrier, 1 + 2 * (ny - 1) + (nz - 1) + (np_ - 1) * nz)
+    pl.semaphore_wait(barrier, 1 + 2 * (ny - 1) + (nz - 1) + (np_ - 1))
+
+    @pl.loop(0, p)
+    def _(q):
+        pl.semaphore_signal(ready.at[p], inc=1, device_id={"row": q, "col": j}, device_id_type=MESH)
 
     def w_y(m, d):
         to = (y + d) % ny
@@ -192,8 +194,6 @@
 
         lcol[z, g] = w[last, g, :, own_columns]
 
-    share(p)
-
     def m_y(d):
         to = (y + d) % ny
         return remote(mw.at[g], mw.at[g], my_s.at[d], my_r.at[y], p, col_of(z, to, c))
@@ -281,32 +281,29 @@
     def _(i):
         across_y(i)
 
-    @pl.loop(0, p - 1)
-    def _(m):
-        share(m)
-
-    @pl.when(p == 0)
-    def _():
-        forward(p)
+    share(p)
+
+    def l_pass_both(k):
+        if k < far:
+
+            @pl.when(p > 0)
+            def _():
+                @pl.loop(0, 2)
+                def _(h):
+                    l_pass(k, h)
+
+    l_pass_both(1)
 
     @pl.loop(0, nz - 1)
     def _(i):
         z_out[i] = across_z(i).astype(BF16)
         z_copy(i).start()
 
-        @pl.when((p > 0) & (i < 2 * far - 2))
-        def _():
-            l_pass(1 + i // 2, i % 2)
-
-    @pl.when(p > 0)
-    def _():
-        forward(p)
-
-    own = across_z(nz - 1)
-    for d in range(1, nz):
-        z_arrival(d).wait_recv()
-        own = own + z_in[(z + d) % nz].astype(F32)
-    res[...] = -own
+    @pl.loop(0, p - 1)
+    def _(m):
+        share(m)
+
+    l_pass_both(2)
 
     def a_copy(d):
         to = (z + d) % nz
@@ -331,17 +328,13 @@
             total = total + dot_t(act[s, src], w[s, :, :, columns].reshape(row_block, row_block))
         return total
 
-    @pl.when(p <= 1)
-    def _():
-        send_current()
+    for k in range(3, far):
+        l_pass_both(k)
 
     @pl.when(p > 0)
     def _():
+        forward(p)
         gathered(p)
-
-        @pl.loop(0, p - 1)
-        def _(m):
-            forward(m)
 
         def columns_of(d):
             return pl.ds(pl.multiple_of(((z + d) % nz) * row_block, row_block), row_block)
@@ -375,6 +368,26 @@
 
         m_c(y).start()
 
+    own = across_z(nz - 1)
+    for d in range(1, nz):
+        z_arrival(d).wait_recv()
+        own = own + z_in[(z + d) % nz].astype(F32)
+    res[...] = -own
+
+    @pl.when(p <= 1)
+    def _():
+        send_current()
+
+    @pl.when(p == 0)
+    def _():
+        forward(p)
+
+    @pl.when(p > 0)
+    def _():
+        @pl.loop(0, p - 1)
+        def _(m):
+            forward(m)
+
         @pl.loop(1, ny)
         def _(d):
             m_y_arrival(d).wait_recv()
@@ -416,6 +429,7 @@
 
     @pl.loop(p + 1, np_)
     def _(q):
+        pl.semaphore_wait(ready.at[q], 1)
         for d in far_first:
             x_copy(q, d).start()
 
@@ -568,6 +582,7 @@
         dma((np_, nz)),
         dma((group,)),
         dma((group,)),
+        pltpu.SemaphoreType.REGULAR((np_,)),
     ]
     anywhere = pl.BlockSpec(memory_space=pl.ANY)
     return pl.pallas_call(

time: 72.7 us -> 69.5 us (0.956)
  Pallas kernels: 71.1 us -> 68 us
    pallas_call x1, Pallas kernels: 71.1 us -> 68 us  [local(): pl.pallas_call(functools.partial(kernel, np_, nz, ny), out_shape=jax.Shap...]
where the time goes in v3:
time: 69.5 us; the launch traced here: 69.4 us
  Pallas kernels  68 us (98%)
  local copies, waits for them, and re-layouts  1.38 us (2%)
    pallas_call x1, Pallas kernels, local(): pl.pallas_call(functools.partial(kernel, np_, nz, ny), out_shape=jax.Shap...  68 us

profile of v3, /device:TPU:7, one launch (start us, length us, event | category | flops | bytes accessed | tf_op | source)
XLA Modules:
  0.0 69.4 jit_solution(11365120662071082264)
XLA Ops:
  0.0 68.0 %shard_map.64 = f32[32,256]{1,0:T(8,128)} custom-call(f32[32,256]{1,0:T(8,128)} %right_ref.1, bf16[2048,256]{1,0:T(8,128)(2,1)} %prior_ref.1, bf16[2048,2048]{1,0:T(8,128)(2,1)} %codes_ref.1, f32[1,8]{1,0:T(1,128)} %scale_ref.1, bf16[1,32,2048]{2,1,0:T(8,128)(2,1)} %diag_ref.1, bf16[1,4,32,2048]{3,2,1,0:T(8,128)(2,1)} %inner_ref.1), custom_call_target="tpu_custom_call" | custom-call | flops 2147483648 | bytes 8388608 | tf_op jit(solution)/shard_map/pallas_call | solution.py:588
  68.0 1.4 %copy.8 = f32[32,256]{1,0:T(8,128)} copy(f32[32,256]{1,0:T(8,128)} %shard_map.64) | data formatting | bytes 65536

commit v4 on v3

--- a/solution.py
+++ b/solution.py
@@ -18,7 +18,7 @@
 def kernel(
     np_, nz, ny,
     right_ref, prior_ref, codes_ref, scale_ref, diag_ref, inner_ref, out_ref,
-    right_v, prior_v, codes_v, prior_t, place, pt, core_out, core_in, half_sum, y_out, y_in, z_out, z_in,
+    right_v, scale_s, prior_v, codes_v, prior_t, place, pt, core_out, core_in, half_sum, y_out, y_in, z_out, z_in,
     w, lcol, macc, mw, act, x_out, res, final_out, final_in,
     in_sem, codes_sem, w_sem, wy_s, wy_r, wc_s, wc_r, la_s, la_r, l_s, l_r, my_s, my_r, mc_s, mc_r, c_s, c_r, y_s, y_r, z_s, z_r, a_s, a_r, x_s, f_s, f_r, ready,
 ):
@@ -33,6 +33,7 @@
     half = right_ref.shape[1] // 2
     chunk = half // ny
     last = jnp.maximum(p - 1, 0)
+    y_near = sorted(range(1, ny), key=lambda d: min(d, ny - d))
     far_first = sorted(range(nz), key=lambda d: -min(d, nz - d))
 
     def col_of(z_, y_, c_):
@@ -65,6 +66,8 @@
 
     load_prior = pltpu.make_async_copy(prior_ref, prior_v, in_sem.at[0])
     load_right = pltpu.make_async_copy(right_ref, right_v, in_sem.at[1])
+    load_scale = pltpu.make_async_copy(scale_ref, scale_s, in_sem.at[2])
+    load_scale.start()
     load_prior.start()
     load_right.start()
 
@@ -89,9 +92,10 @@
 
     load_diag.start()
 
+    load_scale.wait()
     load_prior.wait()
     for b in range(blocks):
-        part = prior_v[b * kb : (b + 1) * kb, :].astype(F32) * scale_ref[0, b]
+        part = prior_v[b * kb : (b + 1) * kb, :].astype(F32) * scale_s[0, b]
         prior_t[:, b * kb : (b + 1) * kb] = part.T.astype(BF16)
     load_right.wait()
     place[...] = jnp.zeros_like(place)
@@ -127,8 +131,7 @@
         load_inner(m).wait()
 
     def share(m):
-        @pl.loop(1, ny)
-        def _(d):
+        for d in y_near:
             w_y(m, d).start()
 
         w_c(m, y).start()
@@ -139,8 +142,7 @@
             w_c_arrival(m, yy).wait_recv()
 
     def forward(m):
-        @pl.loop(1, ny)
-        def _(d):
+        for d in y_near:
             w_y_arrival(m, d).wait_recv()
             w_c(m, (y + d) % ny).start()
 
@@ -267,7 +269,7 @@
         def _():
             across_y(i - lag)
 
-        @pl.when((i == nz // 2) & (p > 0))
+        @pl.when((i == nz // 4) & (p > 0))
         def _():
             @pl.loop(1, group)
             def _(d):
@@ -276,6 +278,14 @@
             @pl.loop(0, 2)
             def _(h):
                 l_start(h)
+
+        if far > 1:
+
+            @pl.when((i == nz - 1) & (p > 0))
+            def _():
+                @pl.loop(0, 2)
+                def _(h):
+                    l_pass(1, h)
 
     @pl.loop(nz - lag, nz)
     def _(i):
@@ -292,19 +302,23 @@
                 def _(h):
                     l_pass(k, h)
 
-    l_pass_both(1)
-
     @pl.loop(0, nz - 1)
     def _(i):
         z_out[i] = across_z(i).astype(BF16)
         z_copy(i).start()
 
+        if far > 2:
+
+            @pl.when((i == nz // 2) & (p > 0))
+            def _():
+                @pl.loop(0, 2)
+                def _(h):
+                    l_pass(2, h)
+
     @pl.loop(0, p - 1)
     def _(m):
         share(m)
 
-    l_pass_both(2)
-
     def a_copy(d):
         to = (z + d) % nz
         return remote(act.at[p, z], act.at[p, z], a_s.at[d], a_r.at[p, z], p, col_of(to, y, c))
@@ -320,7 +334,7 @@
 
     def times(s, own_here):
         total = jnp.zeros((chunk, row_block), F32)
-        for d in range(nz):
+        for d in far_first[::-1]:
             src = (z + d) % nz
             if not (own_here and d == 0):
                 act_arrival(s, src).wait_recv()
@@ -362,8 +376,7 @@
 
         mw[g] = macc[...].astype(BF16)
 
-        @pl.loop(1, ny)
-        def _(d):
+        for d in y_near:
             m_y(d).start()
 
         m_c(y).start()
@@ -388,8 +401,7 @@
         def _(m):
             forward(m)
 
-        @pl.loop(1, ny)
-        def _(d):
+        for d in y_near:
             m_y_arrival(d).wait_recv()
             m_c((y + d) % ny).start()
 
@@ -406,6 +418,49 @@
     def _():
         gathered(p)
 
+    def shared(m):
+        @pl.loop(1, ny)
+        def _(d):
+            w_y(m, d).wait_send()
+
+        @pl.loop(0, ny)
+        def _(yy):
+            w_c(m, yy).wait_send()
+
+    shared(p)
+
+    @pl.loop(0, p - 1)
+    def _(m):
+        shared(m)
+
+    @pl.when(p > 0)
+    def _():
+        @pl.loop(1, group)
+        def _(d):
+            la_copy(d).wait_send()
+
+        @pl.loop(0, 2)
+        def _(h):
+            @pl.loop(1, far + 1)
+            def _(k):
+                l_move(k, h, 0).wait_send()
+
+            @pl.loop(1, far)
+            def _(k):
+                l_move(k, h, 1).wait_send()
+
+    @pl.loop(0, nz)
+    def _(i):
+        core_copy(i).wait_send()
+
+        @pl.loop(1, ny)
+        def _(d):
+            y_copy(i, d).wait_send()
+
+    @pl.loop(0, nz - 1)
+    def _(i):
+        z_copy(i).wait_send()
+
     res[...] = times(p, True)
 
     @pl.when(p > 0)
@@ -415,7 +470,8 @@
             m_c_arrival(yy).wait_recv()
 
         total = jnp.zeros((chunk, row_block), F32)
-        for src in range(nz):
+        for d in far_first[::-1]:
+            src = (z + d) % nz
             act_arrival(last, src).wait_recv()
             total = total + dot_t(act[last, src], mw[src])
         res[...] -= total
@@ -461,37 +517,8 @@
             total = total + final_in[yy * 2 + cc]
         out_ref[:, cc * half : (cc + 1) * half] = total
 
-    def shared(m):
-        @pl.loop(1, ny)
-        def _(d):
-            w_y(m, d).wait_send()
-
-        @pl.loop(0, ny)
-        def _(yy):
-            w_c(m, yy).wait_send()
-
-    shared(p)
-
-    @pl.loop(0, p - 1)
-    def _(m):
-        shared(m)
-
     @pl.when(p > 0)
     def _():
-        @pl.loop(1, group)
-        def _(d):
-            la_copy(d).wait_send()
-
-        @pl.loop(0, 2)
-        def _(h):
-            @pl.loop(1, far + 1)
-            def _(k):
-                l_move(k, h, 0).wait_send()
-
-            @pl.loop(1, far)
-            def _(k):
-                l_move(k, h, 1).wait_send()
-
         @pl.loop(1, ny)
         def _(d):
             m_y(d).wait_send()
@@ -500,18 +527,9 @@
         def _(yy):
             m_c(yy).wait_send()
 
-    @pl.loop(0, nz)
-    def _(i):
-        core_copy(i).wait_send()
-
-        @pl.loop(1, ny)
-        def _(d):
-            y_copy(i, d).wait_send()
-
-    @pl.loop(0, nz - 1)
-    def _(i):
-        z_copy(i).wait_send()
-        a_copy(i + 1).wait_send()
+    @pl.loop(1, nz)
+    def _(d):
+        a_copy(d).wait_send()
 
     @pl.loop(p + 1, np_)
     def _(q):
@@ -535,6 +553,7 @@
     dma = pltpu.SemaphoreType.DMA
     scratch = [
         pltpu.VMEM((rows, rhs), F32),
+        pltpu.SMEM(block_scale.shape, F32),
         pltpu.VMEM((depth, rhs), BF16),
         pltpu.VMEM((nz, row_block, depth), BF16),
         pltpu.VMEM((rhs, depth), BF16),
@@ -556,7 +575,7 @@
         pltpu.VMEM((chunk, row_block), F32),
         pltpu.VMEM((group, rows, half), F32),
         pltpu.VMEM((group, rows, half), F32),
-        dma((2,)),
+        dma((3,)),
         dma((nz,)),
         dma((np_,)),
         dma((np_, ny)),
@@ -588,10 +607,10 @@
     return pl.pallas_call(
         functools.partial(kernel, np_, nz, ny),
         out_shape=jax.ShapeDtypeStruct((rows, rhs), F32),
-        in_specs=[anywhere, anywhere, anywhere, pl.BlockSpec(memory_space=pltpu.SMEM), anywhere, anywhere],
+        in_specs=[anywhere] * 6,
         out_specs=pl.BlockSpec(memory_space=pltpu.VMEM),
         scratch_shapes=scratch,
-        compiler_params=pltpu.CompilerParams(collective_id=0, has_side_effects=True, vmem_limit_bytes=60 * 2**20),
+        compiler_params=pltpu.CompilerParams(collective_id=0, has_side_effects=True, vmem_limit_bytes=54 * 2**20 - 2**17),
         cost_estimate=pl.CostEstimate(
             flops=2 * nz * row_block * depth * rhs, bytes_accessed=2 * nz * row_block * depth, transcendentals=0
         ),

time: 69.5 us -> 67.2 us (0.967)
  Pallas kernels: 68 us -> 65.8 us
    pallas_call x1, Pallas kernels: 68 us -> 65.8 us  [local(): pl.pallas_call(functools.partial(kernel, np_, nz, ny), out_shape=jax.Shap...]
where the time goes in v4:
time: 67.2 us; the launch traced here: 67.1 us
  Pallas kernels  65.8 us (98%)
  local copies, waits for them, and re-layouts  1.27 us (2%)
    pallas_call x1, Pallas kernels, local(): pl.pallas_call(functools.partial(kernel, np_, nz, ny), out_shape=jax.Shap...  65.8 us

profile of v4, /device:TPU:7, one launch (start us, length us, event | category | flops | bytes accessed | tf_op | source)
XLA Modules:
  0.0 67.1 jit_solution(3660018336002732661)
XLA Ops:
  0.0 0.0 copy-start
  0.0 0.7 copy-done
  0.7 65.8 %shard_map.64 = f32[32,256]{1,0:T(8,128)S(1)} custom-call(f32[32,256]{1,0:T(8,128)} %right_ref.1, bf16[2048,256]{1,0:T(8,128)(2,1)} %prior_ref.1, bf16[2048,2048]{1,0:T(8,128)(2,1)} %codes_ref.1, f32[1,8]{1,0:T(1,128)S(1)} %copy-done, bf16[1,32,2048]{2,1,0:T(8,128)(2,1)} %diag_ref.1, bf16[1,4,32,2048]{3,2,1,0:T(8,128)(2,1)} %inner_ref.1), custom_call_target="tpu_custom_call" | custom-call | flops 2147483648 | bytes 8388608 | tf_op jit(solution)/shard_map/pallas_call | solution.py:607
  66.5 0.6 copy.8
Async XLA Ops:
  0.0 0.7 copy-start

commit v5 on v4

--- a/solution.py
+++ b/solution.py
@@ -483,8 +483,9 @@
         to = (z + d) % nz
         return remote(x_out, act.at[p, z], x_s.at[q, d], a_r.at[p, z], q, col_of(to, y, c))
 
-    @pl.loop(p + 1, np_)
-    def _(q):
+    @pl.loop(0, np_ - 1 - p)
+    def _(i):
+        q = np_ - 1 - i
         pl.semaphore_wait(ready.at[q], 1)
         for d in far_first:
             x_copy(q, d).start()

time: 67.2 us -> 65.7 us (0.978)
  Pallas kernels: 65.8 us -> 64.4 us
    pallas_call x1, Pallas kernels: 65.8 us -> 64.4 us  [local(): pl.pallas_call(functools.partial(kernel, np_, nz, ny), out_shape=jax.Shap...]
where the time goes in v5:
time: 65.7 us
  Pallas kernels  64.4 us (98%)
  local copies, waits for them, and re-layouts  1.27 us (2%)
    pallas_call x1, Pallas kernels, local(): pl.pallas_call(functools.partial(kernel, np_, nz, ny), out_shape=jax.Shap...  64.4 us

profile of v5, /device:TPU:7, one launch (start us, length us, event | category | flops | bytes accessed | tf_op | source)
XLA Modules:
  0.0 65.7 jit_solution(13065235940440773573)
XLA Ops:
  0.0 0.0 copy-start
  0.0 0.7 copy-done
  0.7 64.4 %shard_map.64 = f32[32,256]{1,0:T(8,128)S(1)} custom-call(f32[32,256]{1,0:T(8,128)} %right_ref.1, bf16[2048,256]{1,0:T(8,128)(2,1)} %prior_ref.1, bf16[2048,2048]{1,0:T(8,128)(2,1)} %codes_ref.1, f32[1,8]{1,0:T(1,128)S(1)} %copy-done, bf16[1,32,2048]{2,1,0:T(8,128)(2,1)} %diag_ref.1, bf16[1,4,32,2048]{3,2,1,0:T(8,128)(2,1)} %inner_ref.1), custom_call_target="tpu_custom_call" | custom-call | flops 2147483648 | bytes 8388608 | tf_op jit(solution)/shard_map/pallas_call | solution.py:608
  65.0 0.6 copy.8
Async XLA Ops:
  0.0 0.7 copy-start

commit v6 on v5

--- a/solution.py
+++ b/solution.py
@@ -485,7 +485,7 @@
 
     @pl.loop(0, np_ - 1 - p)
     def _(i):
-        q = np_ - 1 - i
+        q = jnp.where(p == 0, 1 + i, np_ - 1 - i)
         pl.semaphore_wait(ready.at[q], 1)
         for d in far_first:
             x_copy(q, d).start()

time: 65.7 us -> 65.7 us (level)
  no operation moved by 1% of the time
where the time goes in v6:
time: 65.7 us
  Pallas kernels  64.4 us (98%)
  local copies, waits for them, and re-layouts  1.27 us (2%)
    pallas_call x1, Pallas kernels, local(): pl.pallas_call(functools.partial(kernel, np_, nz, ny), out_shape=jax.Shap...  64.4 us

profile of v6, /device:TPU:7, one launch (start us, length us, event | category | flops | bytes accessed | tf_op | source)
XLA Modules:
  0.0 65.7 jit_solution(7644474250076401541)
XLA Ops:
  0.0 0.0 copy-start
  0.0 0.7 copy-done
  0.7 64.4 %shard_map.64 = f32[32,256]{1,0:T(8,128)S(1)} custom-call(f32[32,256]{1,0:T(8,128)} %right_ref.1, bf16[2048,256]{1,0:T(8,128)(2,1)} %prior_ref.1, bf16[2048,2048]{1,0:T(8,128)(2,1)} %codes_ref.1, f32[1,8]{1,0:T(1,128)S(1)} %copy-done, bf16[1,32,2048]{2,1,0:T(8,128)(2,1)} %diag_ref.1, bf16[1,4,32,2048]{3,2,1,0:T(8,128)(2,1)} %inner_ref.1), custom_call_target="tpu_custom_call" | custom-call | flops 2147483648 | bytes 8388608 | tf_op jit(solution)/shard_map/pallas_call | solution.py:608
  65.0 0.6 copy.8
Async XLA Ops:
  0.0 0.7 copy-start
